TPU v7x, 32 devices: a whole 2x2x4 slice. The times are simulated.
32 devices in a mesh: gx: 8 (over y, x, core), gy: 4 (over z).
Axes of the slice: x: 2, y: 2, z: 4, core: 2. Of those that a mesh axis runs over, the one named last changes fastest.
Arguments:
- start_block: float32 [8, 8, 512, 512], P(None, None, 'gx', 'gy'), may hold values from -120 to 120
- conductivity: float32 [8, 512, 512], P(None, 'gx', 'gy'), may hold values from 0.5 to 2
- reaction: float32 [8, 512, 512], P(None, 'gx', 'gy'), may hold values from 0.5 to 2
Outputs:
- basis: float32 [40, 8, 512, 512], P(None, None, 'gx', 'gy')
- r_factor: float32 [40, 40], replicated
- first_factor: float32 [40, 40], replicated
All inputs are finite; a program needn't handle non-finite values.
Results may differ from a plain program's by a relative error of at most 0.00045.
Values sent between devices are 32-bit elements; how exact they have to be, the bound alone decides.
A program may use at most 128 MiB of HBM per device.

v0:
```python
import functools

import jax
import jax.numpy as jnp
from jax import lax
from jax.experimental import pallas as pl
from jax.experimental.pallas import tpu as pltpu
from jax.sharding import PartitionSpec as P

STEPS = 4
RHS = 8
NZ = 8
COLS = RHS * (STEPS + 1)
LANES = 128
CENTER_SHIFT = 7.0
THIRD = 1.0 / 3.0
MESH = pl.DeviceIdType.MESH
VM = pl.BlockSpec(memory_space=pltpu.VMEM)
F32 = jnp.float32
BF16 = jnp.bfloat16


def lane_iota(shape):
    return lax.broadcasted_iota(jnp.int32, shape, len(shape) - 1)


def roll(v, shift, axis=1):
    shift = shift % v.shape[axis]
    return v if shift == 0 else pltpu.roll(v, shift, axis)


def pack_kernel(nx, u_ref, c_ref, r_ref, bx, by, bd):
    u2 = u_ref.reshape(RHS * NZ * nx, LANES)
    quad = lane_iota((8, LANES)) // 4
    groups = nx // 4
    tiles = nx // 8

    def group(g, _):
        left = jnp.zeros((8, LANES), F32)
        right = jnp.zeros((8, LANES), F32)
        for j in range(4):
            for z in range(NZ):
                v = u2[pl.ds(z * nx + 4 * g + j, RHS, stride=NZ * nx), :]
                here = quad == 4 * z + j
                left = jnp.where(here, roll(v, 16 * z + 4 * j), left)
                right = jnp.where(here, roll(v, 16 * z + 4 * j + 4), right)
        by[0, g] = left
        by[1, g] = right
        return 0

    lax.fori_loop(0, groups, group, 0)
    for i, ref in enumerate((c_ref, r_ref)):
        for t in range(tiles):
            edge = jnp.zeros((8, LANES), F32)
            for z in range(NZ):
                v = ref[z, 8 * t : 8 * t + 8, :]
                edge = jnp.where(quad == 4 * z + 1, roll(v, 16 * z + 4), edge)
                edge = jnp.where(quad == 4 * z + 2, roll(v, 16 * z + 12), edge)
            by[0, groups + tiles * i + t] = edge
            by[1, groups + tiles * i + t] = edge
    for s in range(2):
        g, t, base = (0, 0, 0) if s == 0 else (groups - 1, tiles - 1, nx - 4)
        for j in range(4):
            for z in range(NZ):
                bx[s, j * 8 + z] = u2[pl.ds(z * nx + base + j, RHS, stride=NZ * nx), :]
        bx[s, 32] = by[0, g]
        bx[s, 33] = by[1, g]
        for z in range(NZ):
            bx[s, 34 + z] = c_ref[z, 8 * t : 8 * t + 8, :]
            bx[s, 42 + z] = r_ref[z, 8 * t : 8 * t + 8, :]
        for i in range(2):
            bx[s, 50 + i] = by[0, groups + tiles * i + t]
        for side in range(2):
            bd[s, side, 0] = by[side, g]
            bd[s, side, 1] = by[0, groups + t]
            bd[s, side, 2] = by[0, groups + tiles + t]


def swap_kernel(gx, gy, bx, by, bd, rx, ry, rd, send, recv):
    mx, my = lax.axis_index("gx"), lax.axis_index("gy")
    xs = (lax.rem(mx + gx - 1, gx), lax.rem(mx + 1, gx))
    ys = (lax.rem(my + gy - 1, gy), lax.rem(my + 1, gy))
    jobs = []
    for s in range(2):
        jobs.append((bx.at[s], rx.at[1 - s], (xs[s], my)))
    for s in range(2):
        jobs.append((by.at[s], ry.at[1 - s], (mx, ys[s])))
    for s in range(2):
        for t in range(2):
            jobs.append((bd.at[s, t], rd.at[1 - s, 1 - t], (xs[s], ys[t])))
    barrier = pltpu.get_barrier_semaphore()
    for _, _, where in jobs:
        pl.semaphore_signal(barrier, inc=1, device_id=where, device_id_type=MESH)
    pl.semaphore_wait(barrier, len(jobs))
    copies = []
    for i, (src, dst, where) in enumerate(jobs):
        copy = pltpu.make_async_remote_copy(
            src_ref=src, dst_ref=dst, send_sem=send.at[i], recv_sem=recv.at[i],
            device_id=where, device_id_type=MESH)
        copy.start()
        copies.append(copy)
    for copy in copies:
        copy.wait()


def split3(a):
    high = a.astype(BF16).astype(F32)
    rest = a - high
    mid = rest.astype(BF16).astype(F32)
    return high, mid, rest - mid


def gram_add(acc, a):
    s = jnp.concatenate(split3(a), 0).astype(BF16)
    acc[...] += lax.dot_general(s, s, (((1,), (1,)), ((), ())), preferred_element_type=F32)


def gram_fold(acc):
    rows = acc[0:COLS, :] + acc[COLS : 2 * COLS, :] + acc[2 * COLS :, :]
    g = rows[:, 0:COLS] + rows[:, COLS : 2 * COLS] + rows[:, 2 * COLS :]
    g = jnp.concatenate([g, jnp.zeros((COLS, LANES - COLS), F32)], 1)
    last = jnp.concatenate([g[32:40], jnp.zeros((8, LANES), F32)], 0)
    return g[0:16] + roll(g[16:32], 40) + roll(last, 80)


def factor(packed, cells):
    g = jnp.concatenate([packed, roll(packed, -40), roll(packed[0:8], -80)], 0) * (1.0 / cells)
    lane = lane_iota((COLS, LANES))
    row = lax.broadcasted_iota(jnp.int32, (COLS, LANES), 0)
    m = jnp.where(lane < COLS, g, jnp.where(lane - 64 == row, 1.0, 0.0))
    row1 = lax.broadcasted_iota(jnp.int32, (COLS, 1), 0)
    for j in range(COLS - 1):
        pivot = m[j : j + 1, :]
        scaled = pivot * (1.0 / m[j : j + 1, j : j + 1])
        f = jnp.where(row1 > j, m[:, j : j + 1], 0.0)
        m = m - f * scaled
    d = jnp.sum(jnp.where(lane == row, m, 0.0), axis=1, keepdims=True)
    m = m * (1.0 / jnp.sqrt(d))
    upper = jnp.where((lane >= row) & (lane < COLS), m, 0.0)
    inverse = jnp.where(lane <= row, roll(m, 64), 0.0)
    return upper[:, :COLS], inverse[:, :COLS]


def stack_left(matrix):
    h, m, l = split3(matrix)
    return jnp.concatenate([h, h, m, m, h, l], 1).astype(BF16)


def times(left, a):
    h, m, l = split3(a)
    hm = jnp.concatenate([h, m], 0).astype(BF16)
    lh = jnp.concatenate([l, h], 0).astype(BF16)
    return jnp.dot(left, jnp.concatenate([hm, hm, lh], 0), preferred_element_type=F32)


def across(ref, i):
    return jnp.concatenate([ref[i, z] for z in range(NZ)], 1)


def power_kernel(nx, u_ref, c_ref, r_ref, by, rx, ry, rd, kb, gp, cb, rb, w, cs, sw, sb, acc):
    ext = nx + 8
    groups = nx // 4
    tiles = nx // 8
    lane = lane_iota((8, LANES))
    lane1 = lane_iota((1, LANES))
    sub = (lane % 16) // 4
    u2 = u_ref.reshape(RHS * NZ * nx, LANES)
    c2 = c_ref.reshape(NZ * nx, LANES)
    r2 = r_ref.reshape(NZ * nx, LANES)
    rx2 = rx.reshape(2 * 52 * 8, LANES)
    W = THIRD * 0.5

    for i, dst in ((0, cb), (1, rb)):
        for k in range(4):
            base = (34 + 8 * i) * 8
            dst[k] = rx2[pl.ds(base + 4 + k, 8, stride=8), :]
            dst[nx + 4 + k] = rx2[pl.ds(52 * 8 + base + k, 8, stride=8), :]

    def coef(x, _):
        cb[x + 4] = c2[pl.ds(x, 8, stride=nx), :]
        rb[x + 4] = r2[pl.ds(x, 8, stride=nx), :]
        for z in range(NZ):
            kb[x + 4, z, 0:RHS, :] = u2[pl.ds(z * nx + x, RHS, stride=NZ * nx), :]
        return 0

    lax.fori_loop(0, nx, coef, 0)
    for j in range(4):
        for z in range(NZ):
            kb[j, z, 0:RHS, :] = rx[0, j * 8 + z]
            kb[nx + 4 + j, z, 0:RHS, :] = rx[1, j * 8 + z]

    w[1, 0] = (cb[0] + cb[1]) * W

    def weight(x, _):
        c = cb[x]
        xp = (c + cb[x + 1]) * W
        zp = (c + roll(c, -1, 0)) * W
        yp = jnp.where(lane == LANES - 1, 0.0, (c + roll(c, -1)) * W)
        zm, ym = roll(zp, 1, 0), roll(yp, 1)
        xm = w[1, x - 1]
        w[0, x] = (rb[x] - CENTER_SHIFT) * THIRD + (xp + xm + zp + zm + yp + ym)
        w[1, x] = xp
        w[2, x] = yp
        w[3, x] = ym
        w[4, x] = zp
        w[5, x] = zm
        return 0

    lax.fori_loop(1, ext - 1, weight, 0)

    for i in range(2):
        cs[i, 0:8, :] = jnp.zeros((8, LANES), F32)
        cs[i, nx + 24 : nx + 32, :] = jnp.zeros((8, LANES), F32)
        for t in range(tiles + 2):
            if t == 0 or t == tiles + 1:
                s = 0 if t == 0 else 1
                own, left, right = rx[s, 50 + i], rd[s, 0, 1 + i], rd[s, 1, 1 + i]
            else:
                at = groups + tiles * i + t - 1
                own, left, right = by[0, at], ry[0, at], ry[1, at]
            cs[i, 8 + 8 * t : 16 + 8 * t, :] = jnp.where(
                sub == 0, roll(left, -8), jnp.where(sub == 3, roll(right, 8), own))
    for t in range(tiles + 2):
        a = 8 + 8 * t
        c = cs[0, a : a + 8, :]
        xp = (c + cs[0, a + 1 : a + 9, :]) * W
        xm = (c + cs[0, a - 1 : a + 7, :]) * W
        yp, ym = (c + roll(c, -1)) * W, (c + roll(c, 1)) * W
        zp, zm = (c + roll(c, -16)) * W, (c + roll(c, 16)) * W
        total = xp + xm + zp + zm + yp + ym
        sw[0, a : a + 8, :] = (cs[1, a : a + 8, :] - CENTER_SHIFT) * THIRD + total
        for k, value in enumerate((xp, xm, yp, ym, zp, zm)):
            sw[1 + k, a : a + 8, :] = value

    def strip(g, parts):
        left, own_left, own_right, right = parts
        for j in range(4):
            v = jnp.where(sub == 0, roll(left, -4 * j), roll(own_left, 4 - 4 * j))
            v = jnp.where(sub == 2, roll(own_right, 8 - 4 * j), v)
            sb[0, 4 * g + j] = jnp.where(sub == 3, roll(right, 12 - 4 * j), v)

    strip(0, (rd[0, 0, 0], rx[0, 32], rx[0, 33], rd[0, 1, 0]))
    strip(groups + 1, (rd[1, 0, 0], rx[1, 32], rx[1, 33], rd[1, 1, 0]))

    def strips(g, _):
        strip(g, (ry[0, g - 1], by[0, g - 1], by[1, g - 1], ry[1, g - 1]))
        return 0

    lax.fori_loop(1, groups + 1, strips, 0)

    acc[...] = jnp.zeros_like(acc)
    edge = (lane == 0) | (lane == LANES - 1)
    for p in range(1, STEPS + 1):
        lo, hi = RHS * (p - 1), RHS * p

        def row(x, _):
            s = sb[p - 1, x]

            def strip_weight(k):
                return sw[k, pl.ds(x + 12, 1), :]

            sr, sl = roll(s, -1), roll(s, 1)
            wr, wl = strip_weight(3), strip_weight(4)
            flux = jnp.where(lane % 16 == 11, wr * (sr - s), roll(wl * (sl - s), 8))
            if p < STEPS:
                sb[p, x] = (
                    strip_weight(0) * s
                    - strip_weight(1) * sb[p - 1, x + 1]
                    - strip_weight(2) * sb[p - 1, x - 1]
                    - wr * sr - wl * sl
                    - strip_weight(5) * roll(s, -16)
                    - strip_weight(6) * roll(s, 16))
            cen = [kb[x, z, lo:hi, :] for z in range(NZ)]
            for z in range(NZ):
                c = cen[z]

                def wt(k, at):
                    return w[k, at, z : z + 1, :]

                new = wt(0, x) * c
                new = new - wt(1, x) * kb[x + 1, z, lo:hi, :]
                new = new - wt(1, x - 1) * kb[x - 1, z, lo:hi, :]
                new = new - wt(2, x) * roll(c, -1)
                new = new - wt(3, x) * roll(c, 1)
                new = new - wt(4, x) * cen[(z + 1) % NZ]
                new = new - wt(5, x) * cen[(z - 1) % NZ]
                new = new - jnp.where(edge, roll(flux, 116 - 16 * z), 0.0)
                kb[x, z, hi : hi + RHS, :] = new
            if p == STEPS:
                gram_add(acc, across(kb, x))
            return 0

        lax.fori_loop(p, ext - p, row, 0)
    gp[...] = gram_fold(acc)


def sum_kernel(gx, gy, g_ref, out, bufx, bufy, sx, rx, sy, ry):
    mx, my = lax.axis_index("gx"), lax.axis_index("gy")
    barrier = pltpu.get_barrier_semaphore()
    xs = [lax.rem(mx + d, gx) for d in range(1, gx)]
    ys = [lax.rem(my + d, gy) for d in range(1, gy)]
    for x in xs:
        pl.semaphore_signal(barrier, inc=1, device_id=(x, my), device_id_type=MESH)
    for y in ys:
        pl.semaphore_signal(barrier, inc=1, device_id=(mx, y), device_id_type=MESH)
    pl.semaphore_wait(barrier, len(xs) + len(ys))

    def stage(source, buf, send, recv, me, n, peers, where):
        copies = []
        for i, peer in enumerate(peers):
            copy = pltpu.make_async_remote_copy(
                src_ref=source, dst_ref=buf.at[me], send_sem=send.at[i],
                recv_sem=recv.at[i], device_id=where(peer), device_id_type=MESH)
            copy.start()
            copies.append(copy)
        buf[me] = source[...]
        for copy in copies:
            copy.wait()
        total = buf[0]
        for i in range(1, n):
            total = total + buf[i]
        return total

    out[...] = stage(g_ref, bufx, sx, rx, mx, gx, xs, lambda x: (x, my))
    out[...] = stage(out, bufy, sy, ry, my, gy, ys, lambda y: (mx, y))


def all_sum(packed, gx, gy, cid):
    return pl.pallas_call(
        functools.partial(sum_kernel, gx, gy),
        out_shape=jax.ShapeDtypeStruct(packed.shape, F32),
        in_specs=[VM],
        out_specs=VM,
        scratch_shapes=[
            pltpu.VMEM((gx,) + packed.shape, F32),
            pltpu.VMEM((gy,) + packed.shape, F32),
            pltpu.SemaphoreType.DMA((gx - 1,)),
            pltpu.SemaphoreType.DMA((gx - 1,)),
            pltpu.SemaphoreType.DMA((gy - 1,)),
            pltpu.SemaphoreType.DMA((gy - 1,)),
        ],
        compiler_params=pltpu.CompilerParams(collective_id=cid, has_side_effects=True),
        name=f"sum_{cid}",
    )(packed)


def again_kernel(cells, steps, g_ref, k_ref, upper, inverse, gp, left, acc):
    i = pl.program_id(0)

    @pl.when(i == 0)
    def _():
        up, inv = factor(g_ref[...], cells)
        upper[...] = up
        inverse[...] = inv
        left[...] = stack_left(inv)
        acc[...] = jnp.zeros_like(acc)

    for x in range(k_ref.shape[0]):
        gram_add(acc, times(left[...], across(k_ref, x)))

    @pl.when(i == steps - 1)
    def _():
        gp[...] = gram_fold(acc)


def basis_kernel(cells, g_ref, up_ref, inv_ref, ka, kc, out, r_out, left):
    @pl.when(pl.program_id(0) == 0)
    def _():
        up, inv = factor(g_ref[...], cells)
        r_out[...] = jnp.dot(up, up_ref[...], precision=lax.Precision.HIGHEST, preferred_element_type=F32)
        both = jnp.dot(inv, inv_ref[...], precision=lax.Precision.HIGHEST, preferred_element_type=F32)
        left[...] = stack_left(both)

    flat = out.reshape(COLS * NZ * 8, LANES)
    for x in range(8):
        ref = ka if x < 4 else kc
        q = times(left[...], across(ref, x % 4))
        for z in range(NZ):
            for b in range(COLS // 8):
                flat[pl.ds(b * 8 * NZ * 8 + z * 8 + x, 8, stride=NZ * 8), :] = q[
                    8 * b : 8 * b + 8, LANES * z : LANES * (z + 1)]


def body(start_block, conductivity, reaction):
    gx, gy = lax.axis_size("gx"), lax.axis_size("gy")
    nx = start_block.shape[2]
    ext = nx + 8
    cells = NZ * nx * LANES * gx * gy
    sds = lambda *s: jax.ShapeDtypeStruct(s, F32)
    shapes = [sds(2, 52, 8, LANES), sds(2, nx // 4 + nx // 4, 8, LANES), sds(2, 2, 3, 8, LANES)]
    big = pltpu.CompilerParams(vmem_limit_bytes=48 * 2**20)
    bx, by, bd = pl.pallas_call(
        functools.partial(pack_kernel, nx), out_shape=shapes,
        in_specs=[VM] * 3, out_specs=[VM] * 3, compiler_params=big, name="pack",
    )(start_block, conductivity, reaction)
    rx, ry, rd = pl.pallas_call(
        functools.partial(swap_kernel, gx, gy), out_shape=shapes,
        in_specs=[VM] * 3, out_specs=[VM] * 3,
        scratch_shapes=[pltpu.SemaphoreType.DMA((8,)), pltpu.SemaphoreType.DMA((8,))],
        compiler_params=pltpu.CompilerParams(collective_id=0, has_side_effects=True), name="swap",
    )(bx, by, bd)
    kb, gp = pl.pallas_call(
        functools.partial(power_kernel, nx),
        out_shape=[sds(ext, NZ, COLS, LANES), sds(16, LANES)],
        in_specs=[VM] * 7, out_specs=[VM] * 2,
        scratch_shapes=[
            pltpu.VMEM((ext, 8, LANES), F32),
            pltpu.VMEM((ext, 8, LANES), F32),
            pltpu.VMEM((6, ext, 8, LANES), F32),
            pltpu.VMEM((2, nx + 32, LANES), F32),
            pltpu.VMEM((7, nx + 32, LANES), F32),
            pltpu.VMEM((STEPS, ext, 8, LANES), F32),
            pltpu.VMEM((3 * COLS, 3 * COLS), F32),
        ],
        compiler_params=big, name="powers",
    )(start_block, conductivity, reaction, by, rx, ry, rd)
    total = all_sum(gp, gx, gy, 1)

    whole = lambda *s: pl.BlockSpec(s, lambda i: (0,) * len(s))
    kblock = lambda f: pl.BlockSpec((4, NZ, COLS, LANES), lambda i: (f(i), 0, 0, 0))
    steps = nx // 4
    upper, inverse, gp2 = pl.pallas_call(
        functools.partial(again_kernel, cells, steps),
        grid=(steps,),
        out_shape=[sds(COLS, COLS), sds(COLS, COLS), sds(16, LANES)],
        in_specs=[whole(16, LANES), kblock(lambda i: i + 1)],
        out_specs=[whole(COLS, COLS), whole(COLS, COLS), whole(16, LANES)],
        scratch_shapes=[pltpu.VMEM((COLS, 6 * COLS), BF16), pltpu.VMEM((3 * COLS, 3 * COLS), F32)],
        compiler_params=big, name="again",
    )(total, kb)
    total2 = all_sum(gp2, gx, gy, 2)
    basis, r_factor = pl.pallas_call(
        functools.partial(basis_kernel, cells),
        grid=(nx // 8,),
        out_shape=[sds(COLS, NZ, nx, LANES), sds(COLS, COLS)],
        in_specs=[whole(16, LANES), whole(COLS, COLS), whole(COLS, COLS),
                  kblock(lambda i: 2 * i + 1), kblock(lambda i: 2 * i + 2)],
        out_specs=[pl.BlockSpec((COLS, NZ, 8, LANES), lambda i: (0, 0, i, 0)), whole(COLS, COLS)],
        scratch_shapes=[pltpu.VMEM((COLS, 6 * COLS), BF16)],
        compiler_params=big, name="basis",
    )(total2, upper, inverse, kb, kb)
    return basis, r_factor, upper


def solution(mesh):
    return jax.shard_map(
        body,
        mesh=mesh,
        in_specs=(P(None, None, "gx", "gy"), P(None, "gx", "gy"), P(None, "gx", "gy")),
        out_specs=(P(None, None, "gx", "gy"), P(), P()),
        check_vma=False,
    )
```

profile of v0, /device:TPU:0, one launch (start us, length us, event | category | flops | bytes accessed | tf_op | source)
XLA Modules:
  0.0 204.7 jit_solution(9274400665627428940)
XLA Ops:
  0.6 0.0 copy-start
  0.6 1.6 copy-done
  2.2 0.0 copy-start.2
  2.2 0.9 copy-done.2
  3.2 0.0 copy-start.4
  3.2 0.9 copy-done.4
  4.1 3.0 %pack.1 = (f32[2,52,8,128]{3,2,1,0:T(8,128)S(1)}, f32[2,32,8,128]{3,2,1,0:T(8,128)S(1)}, f32[2,2,3,8,128]{4,3,2,1,0:T(8,128)S(1)}) custom-call(f32[8,8,64,128]{3,2,1,0:T(8,128)S(1)} %copy-done, f32[8,64,128]{2,1,0:T(8,128)S(1)} %copy-done.2, f32[8,64,128]{2,1,0:T(8,128)S(1)} %copy-done.4), custom_call_target="tpu_custom_call" | custom-call | tf_op jit(solution)/shard_map/pack/pallas_call | solution.py:392
  7.1 0.0 copy-start.6
  7.1 0.7 copy-done.6
  7.8 0.8 copy-done.9
  8.6 0.6 copy-done.12
  9.2 16.7 %swap.1 = (f32[2,52,8,128]{3,2,1,0:T(8,128)}, f32[2,32,8,128]{3,2,1,0:T(8,128)}, f32[2,2,3,8,128]{4,3,2,1,0:T(8,128)}) custom-call(f32[2,52,8,128]{3,2,1,0:T(8,128)} %copy-done.9, f32[2,32,8,128]{3,2,1,0:T(8,128)} %copy-done.6, f32[2,2,3,8,128]{4,3,2,1,0:T(8,128)} %copy-done.12), custom_call_target="tpu_custom_call" | custom-call | tf_op jit(solution)/shard_map/swap/pallas_call | solution.py:396
  25.9 0.0 copy-start.1
  25.9 1.6 copy-done.1
  27.5 0.9 copy-done.3
  28.4 0.9 copy-done.5
  29.4 0.9 copy-done.7
  30.3 1.0 copy-done.8
  31.4 0.9 copy-done.10
  32.3 0.8 copy-done.11
  33.1 104.9 %powers.1 = (f32[72,8,40,128]{3,2,1,0:T(8,128)}, f32[16,128]{1,0:T(8,128)S(1)}) custom-call(f32[8,8,64,128]{3,2,1,0:T(8,128)S(1)} %copy-done.1, f32[8,64,128]{2,1,0:T(8,128)S(1)} %copy-done.3, f32[8,64,128]{2,1,0:T(8,128)S(1)} %copy-done.5, f32[2,32,8,128]{3,2,1,0:T(8,128)S(1)} %copy-done.7, f32[2,52,8,128]{3,2,1,0:T(8,128)S(1)} %copy-done.8, ...), custom_call_target="tpu_custom_call" | custom-call | tf_op jit(solution)/shard_map/powers/pallas_call | solution.py:402
  138.0 0.6 copy-done.16
  138.6 11.1 %sum_1.1.g_ref = f32[16,128]{1,0:T(8,128)} custom-call(f32[16,128]{1,0:T(8,128)} %copy-done.16), custom_call_target="tpu_custom_call" | custom-call | tf_op jit(solution)/shard_map/sum_1/pallas_call | solution.py:329
  149.8 0.0 copy-start.14
  149.8 0.7 copy-done.14
  150.4 24.2 %again.1 = (f32[40,40]{1,0:T(8,128)}, f32[40,40]{1,0:T(8,128)S(1)}, f32[16,128]{1,0:T(8,128)S(1)}) custom-call(f32[16,128]{1,0:T(8,128)S(1)} %copy-done.14, f32[72,8,40,128]{3,2,1,0:T(8,128)} %get-tuple-element.23.k_ref.ka.kc), custom_call_target="tpu_custom_call" | custom-call | tf_op jit(solution)/shard_map/again/pallas_call | solution.py:422
  174.6 0.6 copy-done.17
  175.2 10.3 %sum_2.1.g_ref = f32[16,128]{1,0:T(8,128)} custom-call(f32[16,128]{1,0:T(8,128)} %copy-done.17), custom_call_target="tpu_custom_call" | custom-call | tf_op jit(solution)/shard_map/sum_2/pallas_call | solution.py:329
  185.5 0.0 copy-start.13
  185.5 0.7 copy-done.13
  186.2 0.7 copy-done.15
  186.9 17.7 %basis.1 = (f32[40,8,64,128]{3,2,1,0:T(8,128)}, f32[40,40]{1,0:T(8,128)}) custom-call(f32[16,128]{1,0:T(8,128)S(1)} %copy-done.13, f32[40,40]{1,0:T(8,128)S(1)} %copy-done.15, f32[40,40]{1,0:T(8,128)S(1)} %get-tuple-element.26.inv_ref, f32[72,8,40,128]{3,2,1,0:T(8,128)} %get-tuple-element.23.k_ref.ka.kc, f32[72,8,40,128]{3,2,1,0:T(8,128)} %get-tuple-element.23.k_ref.ka.kc), custom_call_target="tpu_custom_call" | custom-call | tf_op jit(solution)/shard_map/basis/pallas_call | solution.py:432
  (11 shorter events, 0.0 us)
Async XLA Ops:
  0.6 1.6 copy-start
  2.2 0.9 copy-start.2
  3.2 0.9 copy-start.4
  7.1 0.7 copy-start.6
  7.8 0.8 copy-start.9
  8.6 0.6 copy-start.12
  25.9 1.6 copy-start.1
  27.5 0.9 copy-start.3
  28.4 0.9 copy-start.5
  29.4 0.9 copy-start.7
  30.3 1.0 copy-start.8
  31.4 0.9 copy-start.10
  32.3 0.8 copy-start.11
  138.0 0.6 copy-start.16
  149.8 0.7 copy-start.14
  174.6 0.6 copy-start.17
  185.5 0.7 copy-start.13
  186.2 0.7 copy-start.15
where the time goes:
time: 206 us; the launch traced here: 205 us
  Pallas kernels  188 us (91%)
  local copies, waits for them, and re-layouts  16 us (8%)
    pallas_call x1, Pallas kernels, body(): pl.pallas_call(functools.partial(power_kernel, nx), out_shape=[sds(ext, N...  105 us
    pallas_call x1, Pallas kernels, body(): pl.pallas_call(functools.partial(again_kernel, cells, steps), grid=(steps...  24.2 us
    pallas_call x2, Pallas kernels, all_sum(): pl.pallas_call(functools.partial(sum_kernel, gx, gy), out_shape=jax.Shape...  21.5 us
    pallas_call x1, Pallas kernels, body(): pl.pallas_call(functools.partial(basis_kernel, cells), grid=(nx // 8,), o...  17.7 us
    pallas_call x1, Pallas kernels, body(): pl.pallas_call(functools.partial(swap_kernel, gx, gy), out_shape=shapes,...  16.7 us
    unnamed x36, local copies, waits for them, and re-layouts  16 us

commit v1 on v0

--- a/solution.py
+++ b/solution.py
@@ -153,11 +153,15 @@
     return jnp.dot(left, jnp.concatenate([hm, hm, lh], 0), preferred_element_type=F32)
 
 
-def across(ref, i):
-    return jnp.concatenate([ref[i, z] for z in range(NZ)], 1)
-
-
-def power_kernel(nx, u_ref, c_ref, r_ref, by, rx, ry, rd, kb, gp, cb, rb, w, cs, sw, sb, acc):
+def across(ref, rows):
+    return jnp.concatenate([ref[i, z] for i in rows for z in range(NZ)], 1)
+
+
+def rows_at_once(count, most):
+    return max(n for n in range(1, most + 1) if count % n == 0)
+
+
+def power_kernel(nx, u_ref, c_ref, r_ref, by, rx, ry, rd, out, gp, kb, cb, rb, w, cs, sw, sb, fl, acc, sem):
     ext = nx + 8
     groups = nx // 4
     tiles = nx // 8
@@ -176,14 +180,18 @@
             dst[k] = rx2[pl.ds(base + 4 + k, 8, stride=8), :]
             dst[nx + 4 + k] = rx2[pl.ds(52 * 8 + base + k, 8, stride=8), :]
 
-    def coef(x, _):
-        cb[x + 4] = c2[pl.ds(x, 8, stride=nx), :]
-        rb[x + 4] = r2[pl.ds(x, 8, stride=nx), :]
-        for z in range(NZ):
-            kb[x + 4, z, 0:RHS, :] = u2[pl.ds(z * nx + x, RHS, stride=NZ * nx), :]
+    def coef(i, _):
+        xs = [4 * i + k for k in range(4)]
+        cr = [(c2[pl.ds(x, 8, stride=nx), :], r2[pl.ds(x, 8, stride=nx), :]) for x in xs]
+        us = [[u2[pl.ds(z * nx + x, RHS, stride=NZ * nx), :] for z in range(NZ)] for x in xs]
+        for k, x in enumerate(xs):
+            cb[x + 4] = cr[k][0]
+            rb[x + 4] = cr[k][1]
+            for z in range(NZ):
+                kb[x + 4, z, 0:RHS, :] = us[k][z]
         return 0
 
-    lax.fori_loop(0, nx, coef, 0)
+    lax.fori_loop(0, nx // 4, coef, 0)
     for j in range(4):
         for z in range(NZ):
             kb[j, z, 0:RHS, :] = rx[0, j * 8 + z]
@@ -191,22 +199,26 @@
 
     w[1, 0] = (cb[0] + cb[1]) * W
 
-    def weight(x, _):
-        c = cb[x]
-        xp = (c + cb[x + 1]) * W
-        zp = (c + roll(c, -1, 0)) * W
-        yp = jnp.where(lane == LANES - 1, 0.0, (c + roll(c, -1)) * W)
-        zm, ym = roll(zp, 1, 0), roll(yp, 1)
-        xm = w[1, x - 1]
-        w[0, x] = (rb[x] - CENTER_SHIFT) * THIRD + (xp + xm + zp + zm + yp + ym)
-        w[1, x] = xp
-        w[2, x] = yp
-        w[3, x] = ym
-        w[4, x] = zp
-        w[5, x] = zm
+    many = rows_at_once(ext - 2, 10)
+
+    def weight(i, _):
+        out = []
+        for k in range(many):
+            x = 1 + i * many + k
+            c = cb[x]
+            xp, xm = (c + cb[x + 1]) * W, (c + cb[x - 1]) * W
+            zp = (c + roll(c, -1, 0)) * W
+            yp = jnp.where(lane == LANES - 1, 0.0, (c + roll(c, -1)) * W)
+            zm = roll(zp, 1, 0)
+            ym = jnp.where(lane == 0, 0.0, (c + roll(c, 1)) * W)
+            diag = (rb[x] - CENTER_SHIFT) * THIRD + (xp + xm + zp + zm + yp + ym)
+            out.append((diag, xp, yp, ym, zp, zm))
+        for k in range(many):
+            for n in range(6):
+                w[n, 1 + i * many + k] = out[k][n]
         return 0
 
-    lax.fori_loop(1, ext - 1, weight, 0)
+    lax.fori_loop(0, (ext - 2) // many, weight, 0)
 
     for i in range(2):
         cs[i, 0:8, :] = jnp.zeros((8, LANES), F32)
@@ -248,50 +260,75 @@
 
     lax.fori_loop(1, groups + 1, strips, 0)
 
+    for p in range(STEPS):
+        size = rows_at_once(ext - 2 * p - 2, 17)
+
+        def strip_rows(i, _):
+            fluxes, nexts = [], []
+            for k in range(size):
+                x = p + 1 + i * size + k
+                s = sb[p, x]
+
+                def wt(n):
+                    return sw[n, pl.ds(x + 12, 1), :]
+
+                sr, sl = roll(s, -1), roll(s, 1)
+                wr, wl = wt(3), wt(4)
+                fluxes.append(jnp.where(lane % 16 == 11, wr * (sr - s), roll(wl * (sl - s), 8)))
+                if p < STEPS - 1:
+                    ax = wt(1) * sb[p, x + 1] + wt(2) * sb[p, x - 1]
+                    az = wt(5) * roll(s, -16) + wt(6) * roll(s, 16)
+                    nexts.append((wt(0) * s - ax) - ((wr * sr + wl * sl) + az))
+            for k in range(size):
+                x = p + 1 + i * size + k
+                fl[p, x] = fluxes[k]
+                if p < STEPS - 1:
+                    sb[p + 1, x] = nexts[k]
+            return 0
+
+        lax.fori_loop(0, (ext - 2 * p - 2) // size, strip_rows, 0)
+
     acc[...] = jnp.zeros_like(acc)
     edge = (lane == 0) | (lane == LANES - 1)
+
+    def leave(i, count):
+        return pltpu.make_async_copy(
+            kb.at[pl.ds(4 + i * count, count)], out.at[pl.ds(i * count, count)], sem.at[i])
+
     for p in range(1, STEPS + 1):
         lo, hi = RHS * (p - 1), RHS * p
-
-        def row(x, _):
-            s = sb[p - 1, x]
-
-            def strip_weight(k):
-                return sw[k, pl.ds(x + 12, 1), :]
-
-            sr, sl = roll(s, -1), roll(s, 1)
-            wr, wl = strip_weight(3), strip_weight(4)
-            flux = jnp.where(lane % 16 == 11, wr * (sr - s), roll(wl * (sl - s), 8))
-            if p < STEPS:
-                sb[p, x] = (
-                    strip_weight(0) * s
-                    - strip_weight(1) * sb[p - 1, x + 1]
-                    - strip_weight(2) * sb[p - 1, x - 1]
-                    - wr * sr - wl * sl
-                    - strip_weight(5) * roll(s, -16)
-                    - strip_weight(6) * roll(s, 16))
-            cen = [kb[x, z, lo:hi, :] for z in range(NZ)]
-            for z in range(NZ):
-                c = cen[z]
-
-                def wt(k, at):
-                    return w[k, at, z : z + 1, :]
-
-                new = wt(0, x) * c
-                new = new - wt(1, x) * kb[x + 1, z, lo:hi, :]
-                new = new - wt(1, x - 1) * kb[x - 1, z, lo:hi, :]
-                new = new - wt(2, x) * roll(c, -1)
-                new = new - wt(3, x) * roll(c, 1)
-                new = new - wt(4, x) * cen[(z + 1) % NZ]
-                new = new - wt(5, x) * cen[(z - 1) % NZ]
-                new = new - jnp.where(edge, roll(flux, 116 - 16 * z), 0.0)
-                kb[x, z, hi : hi + RHS, :] = new
+        count = rows_at_once(ext - 2 * p, 5)
+
+        def rows(i, _):
+            first = p + i * count
+            news = {}
+            for k in range(count):
+                x = first + k
+                cen = [kb[x, z, lo:hi, :] for z in range(NZ)]
+                flux = fl[p - 1, x]
+                for z in range(NZ):
+                    c = cen[z]
+
+                    def wt(n, at):
+                        return w[n, at, z : z + 1, :]
+
+                    mid = wt(0, x) * c - jnp.where(edge, roll(flux, 116 - 16 * z), 0.0)
+                    ax = wt(1, x) * kb[x + 1, z, lo:hi, :] + wt(1, x - 1) * kb[x - 1, z, lo:hi, :]
+                    ay = wt(2, x) * roll(c, -1) + wt(3, x) * roll(c, 1)
+                    az = wt(4, x) * cen[(z + 1) % NZ] + wt(5, x) * cen[(z - 1) % NZ]
+                    news[k, z] = (mid - ax) - (ay + az)
+            for k in range(count):
+                for z in range(NZ):
+                    kb[first + k, z, hi : hi + RHS, :] = news[k, z]
             if p == STEPS:
-                gram_add(acc, across(kb, x))
+                leave(i, count).start()
+                gram_add(acc, across(kb, [first + k for k in range(count)]))
             return 0
 
-        lax.fori_loop(p, ext - p, row, 0)
+        lax.fori_loop(0, (ext - 2 * p) // count, rows, 0)
     gp[...] = gram_fold(acc)
+    for i in range(nx // 4):
+        leave(i, 4).wait()
 
 
 def sum_kernel(gx, gy, g_ref, out, bufx, bufy, sx, rx, sy, ry):
@@ -355,15 +392,14 @@
         left[...] = stack_left(inv)
         acc[...] = jnp.zeros_like(acc)
 
-    for x in range(k_ref.shape[0]):
-        gram_add(acc, times(left[...], across(k_ref, x)))
+    gram_add(acc, times(left[...], across(k_ref, range(k_ref.shape[0]))))
 
     @pl.when(i == steps - 1)
     def _():
         gp[...] = gram_fold(acc)
 
 
-def basis_kernel(cells, g_ref, up_ref, inv_ref, ka, kc, out, r_out, left):
+def basis_kernel(cells, g_ref, up_ref, inv_ref, k_ref, out, r_out, left):
     @pl.when(pl.program_id(0) == 0)
     def _():
         up, inv = factor(g_ref[...], cells)
@@ -373,8 +409,7 @@
 
     flat = out.reshape(COLS * NZ * 8, LANES)
     for x in range(8):
-        ref = ka if x < 4 else kc
-        q = times(left[...], across(ref, x % 4))
+        q = times(left[...], across(k_ref, [x]))
         for z in range(NZ):
             for b in range(COLS // 8):
                 flat[pl.ds(b * 8 * NZ * 8 + z * 8 + x, 8, stride=NZ * 8), :] = q[
@@ -401,29 +436,32 @@
     )(bx, by, bd)
     kb, gp = pl.pallas_call(
         functools.partial(power_kernel, nx),
-        out_shape=[sds(ext, NZ, COLS, LANES), sds(16, LANES)],
-        in_specs=[VM] * 7, out_specs=[VM] * 2,
+        out_shape=[sds(nx, NZ, COLS, LANES), sds(16, LANES)],
+        in_specs=[VM] * 7, out_specs=[pl.BlockSpec(memory_space=pl.ANY), VM],
         scratch_shapes=[
+            pltpu.VMEM((ext, NZ, COLS, LANES), F32),
             pltpu.VMEM((ext, 8, LANES), F32),
             pltpu.VMEM((ext, 8, LANES), F32),
             pltpu.VMEM((6, ext, 8, LANES), F32),
             pltpu.VMEM((2, nx + 32, LANES), F32),
             pltpu.VMEM((7, nx + 32, LANES), F32),
             pltpu.VMEM((STEPS, ext, 8, LANES), F32),
+            pltpu.VMEM((STEPS, ext, 8, LANES), F32),
             pltpu.VMEM((3 * COLS, 3 * COLS), F32),
+            pltpu.SemaphoreType.DMA((nx // 4,)),
         ],
         compiler_params=big, name="powers",
     )(start_block, conductivity, reaction, by, rx, ry, rd)
     total = all_sum(gp, gx, gy, 1)
 
     whole = lambda *s: pl.BlockSpec(s, lambda i: (0,) * len(s))
-    kblock = lambda f: pl.BlockSpec((4, NZ, COLS, LANES), lambda i: (f(i), 0, 0, 0))
+    kblock = lambda n: pl.BlockSpec((n, NZ, COLS, LANES), lambda i: (i, 0, 0, 0))
     steps = nx // 4
     upper, inverse, gp2 = pl.pallas_call(
         functools.partial(again_kernel, cells, steps),
         grid=(steps,),
         out_shape=[sds(COLS, COLS), sds(COLS, COLS), sds(16, LANES)],
-        in_specs=[whole(16, LANES), kblock(lambda i: i + 1)],
+        in_specs=[whole(16, LANES), kblock(4)],
         out_specs=[whole(COLS, COLS), whole(COLS, COLS), whole(16, LANES)],
         scratch_shapes=[pltpu.VMEM((COLS, 6 * COLS), BF16), pltpu.VMEM((3 * COLS, 3 * COLS), F32)],
         compiler_params=big, name="again",
@@ -434,11 +472,11 @@
         grid=(nx // 8,),
         out_shape=[sds(COLS, NZ, nx, LANES), sds(COLS, COLS)],
         in_specs=[whole(16, LANES), whole(COLS, COLS), whole(COLS, COLS),
-                  kblock(lambda i: 2 * i + 1), kblock(lambda i: 2 * i + 2)],
+                  kblock(8)],
         out_specs=[pl.BlockSpec((COLS, NZ, 8, LANES), lambda i: (0, 0, i, 0)), whole(COLS, COLS)],
         scratch_shapes=[pltpu.VMEM((COLS, 6 * COLS), BF16)],
         compiler_params=big, name="basis",
-    )(total2, upper, inverse, kb, kb)
+    )(total2, upper, inverse, kb)
     return basis, r_factor, upper
 
 

time: 206 us -> 123 us (0.60)
  Pallas kernels: 188 us -> 105 us
    pallas_call x1, Pallas kernels: 105 us -> 25.5 us  [body(): pl.pallas_call(functools.partial(power_kernel, nx), out_shape=[sds(nx, NZ...]
    pallas_call x1, Pallas kernels: 24.2 us -> 20.7 us  [body(): pl.pallas_call(functools.partial(again_kernel, cells, steps), grid=(steps...]
where the time goes in v1:
time: 123 us; the launch traced here: 122 us
  Pallas kernels  105 us (85%)
  local copies, waits for them, and re-layouts  16 us (13%)
    pallas_call x1, Pallas kernels, body(): pl.pallas_call(functools.partial(power_kernel, nx), out_shape=[sds(nx, NZ...  25.5 us
    pallas_call x2, Pallas kernels, all_sum(): pl.pallas_call(functools.partial(sum_kernel, gx, gy), out_shape=jax.Shape...  21.5 us
    pallas_call x1, Pallas kernels, body(): pl.pallas_call(functools.partial(again_kernel, cells, steps), grid=(steps...  20.7 us
    pallas_call x1, Pallas kernels, body(): pl.pallas_call(functools.partial(basis_kernel, cells), grid=(nx // 8,), o...  17.8 us
    pallas_call x1, Pallas kernels, body(): pl.pallas_call(functools.partial(swap_kernel, gx, gy), out_shape=shapes,...  16.7 us
    unnamed x36, local copies, waits for them, and re-layouts  16 us
    pallas_call x1, Pallas kernels, body(): pl.pallas_call(functools.partial(pack_kernel, nx), out_shape=shapes, in_s...  2.96 us

profile of v1, /device:TPU:0, one launch (start us, length us, event | category | flops | bytes accessed | tf_op | source)
XLA Modules:
  0.0 122.0 jit_solution(11300382822847886445)
XLA Ops:
  0.6 0.0 copy-start
  0.6 1.6 %copy-done = f32[8,8,64,128]{3,2,1,0:T(8,128)S(1)} copy-done((f32[8,8,64,128]{3,2,1,0:T(8,128)S(1)}, f32[8,8,64,128]{3,2,1,0:T(8,128)}, u32[]{:S(2)}) %copy-start) | copy-done | bytes 2097176
  2.2 0.0 copy-start.2
  2.2 0.9 copy-done.2
  3.2 0.9 copy-done.4
  4.1 3.0 %pack.1 = (f32[2,52,8,128]{3,2,1,0:T(8,128)S(1)}, f32[2,32,8,128]{3,2,1,0:T(8,128)S(1)}, f32[2,2,3,8,128]{4,3,2,1,0:T(8,128)S(1)}) custom-call(f32[8,8,64,128]{3,2,1,0:T(8,128)S(1)} %copy-done, f32[8,64,128]{2,1,0:T(8,128)S(1)} %copy-done.2, f32[8,64,128]{2,1,0:T(8,128)S(1)} %copy-done.4), custom_call_target="tpu_custom_call" | custom-call | tf_op jit(solution)/shard_map/pack/pallas_call | solution.py:427
  7.1 0.0 copy-start.6
  7.1 0.7 copy-done.6
  7.8 0.8 copy-done.9
  8.6 0.6 copy-done.12
  9.2 16.7 %swap.1 = (f32[2,52,8,128]{3,2,1,0:T(8,128)}, f32[2,32,8,128]{3,2,1,0:T(8,128)}, f32[2,2,3,8,128]{4,3,2,1,0:T(8,128)}) custom-call(f32[2,52,8,128]{3,2,1,0:T(8,128)} %copy-done.9, f32[2,32,8,128]{3,2,1,0:T(8,128)} %copy-done.6, f32[2,2,3,8,128]{4,3,2,1,0:T(8,128)} %copy-done.12), custom_call_target="tpu_custom_call" | custom-call | tf_op jit(solution)/shard_map/swap/pallas_call | solution.py:431
  25.9 0.0 copy-start.1
  25.9 1.6 %copy-done.1 = f32[8,8,64,128]{3,2,1,0:T(8,128)S(1)} copy-done((f32[8,8,64,128]{3,2,1,0:T(8,128)S(1)}, f32[8,8,64,128]{3,2,1,0:T(8,128)}, u32[]{:S(2)}) %copy-start.1) | copy-done | bytes 2097176
  27.5 0.9 copy-done.3
  28.4 0.9 copy-done.5
  29.4 0.9 copy-done.7
  30.3 1.0 copy-done.8
  31.4 0.9 copy-done.10
  32.3 0.8 copy-done.11
  33.1 25.5 %powers.1 = (f32[64,8,40,128]{3,2,1,0:T(8,128)}, f32[16,128]{1,0:T(8,128)S(1)}) custom-call(f32[8,8,64,128]{3,2,1,0:T(8,128)S(1)} %copy-done.1, f32[8,64,128]{2,1,0:T(8,128)S(1)} %copy-done.3, f32[8,64,128]{2,1,0:T(8,128)S(1)} %copy-done.5, f32[2,32,8,128]{3,2,1,0:T(8,128)S(1)} %copy-done.7, f32[2,52,8,128]{3,2,1,0:T(8,128)S(1)} %copy-done.8, ...), custom_call_target="tpu_custom_call" | custom-call | tf_op jit(solution)/shard_map/powers/pallas_call | solution.py:437
  58.6 0.0 copy-start.16
  58.6 0.6 copy-done.16
  59.2 11.2 %sum_1.1.g_ref = f32[16,128]{1,0:T(8,128)} custom-call(f32[16,128]{1,0:T(8,128)} %copy-done.16), custom_call_target="tpu_custom_call" | custom-call | tf_op jit(solution)/shard_map/sum_1/pallas_call | solution.py:366
  70.4 0.0 copy-start.14
  70.4 0.7 copy-done.14
  71.1 20.7 %again.1 = (f32[40,40]{1,0:T(8,128)}, f32[40,40]{1,0:T(8,128)S(1)}, f32[16,128]{1,0:T(8,128)S(1)}) custom-call(f32[16,128]{1,0:T(8,128)S(1)} %copy-done.14, f32[64,8,40,128]{3,2,1,0:T(8,128)} %get-tuple-element.23.k_ref), custom_call_target="tpu_custom_call" | custom-call | tf_op jit(solution)/shard_map/again/pallas_call | solution.py:460
  91.8 0.6 copy-done.17
  92.4 10.3 %sum_2.1.g_ref = f32[16,128]{1,0:T(8,128)} custom-call(f32[16,128]{1,0:T(8,128)} %copy-done.17), custom_call_target="tpu_custom_call" | custom-call | tf_op jit(solution)/shard_map/sum_2/pallas_call | solution.py:366
  102.7 0.0 copy-start.13
  102.7 0.7 copy-done.13
  103.4 0.7 copy-done.15
  104.1 17.8 %basis.1 = (f32[40,8,64,128]{3,2,1,0:T(8,128)}, f32[40,40]{1,0:T(8,128)}) custom-call(f32[16,128]{1,0:T(8,128)S(1)} %copy-done.13, f32[40,40]{1,0:T(8,128)S(1)} %copy-done.15, f32[40,40]{1,0:T(8,128)S(1)} %get-tuple-element.26.inv_ref, f32[64,8,40,128]{3,2,1,0:T(8,128)} %get-tuple-element.23.k_ref), custom_call_target="tpu_custom_call" | custom-call | tf_op jit(solution)/shard_map/basis/pallas_call | solution.py:470
  (11 shorter events, 0.0 us)
Async XLA Ops:
  0.6 1.6 %copy-start = (f32[8,8,64,128]{3,2,1,0:T(8,128)S(1)}, f32[8,8,64,128]{3,2,1,0:T(8,128)}, u32[]{:S(2)}) copy-start(f32[8,8,64,128]{3,2,1,0:T(8,128)} %u_ref.3) | copy-start | bytes 6291460
  2.2 0.9 copy-start.2
  3.2 0.9 copy-start.4
  7.1 0.7 copy-start.6
  7.8 0.8 copy-start.9
  8.6 0.6 copy-start.12
  25.9 1.6 %copy-start.1 = (f32[8,8,64,128]{3,2,1,0:T(8,128)S(1)}, f32[8,8,64,128]{3,2,1,0:T(8,128)}, u32[]{:S(2)}) copy-start(f32[8,8,64,128]{3,2,1,0:T(8,128)} %u_ref.3) | copy-start | bytes 6291460
  27.5 0.9 copy-start.3
  28.4 0.9 copy-start.5
  29.4 0.9 copy-start.7
  30.3 1.0 copy-start.8
  31.4 0.9 copy-start.10
  32.3 0.8 copy-start.11
  58.6 0.6 copy-start.16
  70.4 0.7 copy-start.14
  91.8 0.6 copy-start.17
  102.7 0.7 copy-start.13
  103.4 0.7 copy-start.15

commit v2 on v1

--- a/solution.py
+++ b/solution.py
@@ -297,7 +297,7 @@
 
     for p in range(1, STEPS + 1):
         lo, hi = RHS * (p - 1), RHS * p
-        count = rows_at_once(ext - 2 * p, 5)
+        count = 4 if p == STEPS else rows_at_once(ext - 2 * p, 6)
 
         def rows(i, _):
             first = p + i * count
@@ -392,7 +392,8 @@
         left[...] = stack_left(inv)
         acc[...] = jnp.zeros_like(acc)
 
-    gram_add(acc, times(left[...], across(k_ref, range(k_ref.shape[0]))))
+    for first in range(0, k_ref.shape[0], 4):
+        gram_add(acc, times(left[...], across(k_ref, range(first, first + 4))))
 
     @pl.when(i == steps - 1)
     def _():
@@ -456,12 +457,12 @@
 
     whole = lambda *s: pl.BlockSpec(s, lambda i: (0,) * len(s))
     kblock = lambda n: pl.BlockSpec((n, NZ, COLS, LANES), lambda i: (i, 0, 0, 0))
-    steps = nx // 4
+    steps = nx // 8
     upper, inverse, gp2 = pl.pallas_call(
         functools.partial(again_kernel, cells, steps),
         grid=(steps,),
         out_shape=[sds(COLS, COLS), sds(COLS, COLS), sds(16, LANES)],
-        in_specs=[whole(16, LANES), kblock(4)],
+        in_specs=[whole(16, LANES), kblock(8)],
         out_specs=[whole(COLS, COLS), whole(COLS, COLS), whole(16, LANES)],
         scratch_shapes=[pltpu.VMEM((COLS, 6 * COLS), BF16), pltpu.VMEM((3 * COLS, 3 * COLS), F32)],
         compiler_params=big, name="again",

time: 123 us -> 119 us (0.967)
  Pallas kernels: 105 us -> 101 us
    pallas_call x1, Pallas kernels: 20.7 us -> 17.7 us  [body(): pl.pallas_call(functools.partial(again_kernel, cells, steps), grid=(steps...]
where the time goes in v2:
time: 119 us; the launch traced here: 118 us
  Pallas kernels  101 us (85%)
  local copies, waits for them, and re-layouts  16 us (13%)
    pallas_call x1, Pallas kernels, body(): pl.pallas_call(functools.partial(power_kernel, nx), out_shape=[sds(nx, NZ...  24.7 us
    pallas_call x2, Pallas kernels, all_sum(): pl.pallas_call(functools.partial(sum_kernel, gx, gy), out_shape=jax.Shape...  21.5 us
    pallas_call x1, Pallas kernels, body(): pl.pallas_call(functools.partial(basis_kernel, cells), grid=(nx // 8,), o...  17.8 us
    pallas_call x1, Pallas kernels, body(): pl.pallas_call(functools.partial(again_kernel, cells, steps), grid=(steps...  17.7 us
    pallas_call x1, Pallas kernels, body(): pl.pallas_call(functools.partial(swap_kernel, gx, gy), out_shape=shapes,...  16.7 us
    unnamed x36, local copies, waits for them, and re-layouts  16 us
    pallas_call x1, Pallas kernels, body(): pl.pallas_call(functools.partial(pack_kernel, nx), out_shape=shapes, in_s...  2.96 us

profile of v2, /device:TPU:0, one launch (start us, length us, event | category | flops | bytes accessed | tf_op | source)
XLA Modules:
  0.0 118.2 jit_solution(1380121985434186901)
XLA Ops:
  0.6 0.0 copy-start
  0.6 1.6 %copy-done = f32[8,8,64,128]{3,2,1,0:T(8,128)S(1)} copy-done((f32[8,8,64,128]{3,2,1,0:T(8,128)S(1)}, f32[8,8,64,128]{3,2,1,0:T(8,128)}, u32[]{:S(2)}) %copy-start) | copy-done | bytes 2097176
  2.2 0.0 copy-start.2
  2.2 0.9 copy-done.2
  3.2 0.9 copy-done.4
  4.1 3.0 %pack.1 = (f32[2,52,8,128]{3,2,1,0:T(8,128)S(1)}, f32[2,32,8,128]{3,2,1,0:T(8,128)S(1)}, f32[2,2,3,8,128]{4,3,2,1,0:T(8,128)S(1)}) custom-call(f32[8,8,64,128]{3,2,1,0:T(8,128)S(1)} %copy-done, f32[8,64,128]{2,1,0:T(8,128)S(1)} %copy-done.2, f32[8,64,128]{2,1,0:T(8,128)S(1)} %copy-done.4), custom_call_target="tpu_custom_call" | custom-call | tf_op jit(solution)/shard_map/pack/pallas_call | solution.py:428
  7.1 0.0 copy-start.6
  7.1 0.7 copy-done.6
  7.8 0.8 copy-done.9
  8.6 0.6 copy-done.12
  9.2 16.7 %swap.1 = (f32[2,52,8,128]{3,2,1,0:T(8,128)}, f32[2,32,8,128]{3,2,1,0:T(8,128)}, f32[2,2,3,8,128]{4,3,2,1,0:T(8,128)}) custom-call(f32[2,52,8,128]{3,2,1,0:T(8,128)} %copy-done.9, f32[2,32,8,128]{3,2,1,0:T(8,128)} %copy-done.6, f32[2,2,3,8,128]{4,3,2,1,0:T(8,128)} %copy-done.12), custom_call_target="tpu_custom_call" | custom-call | tf_op jit(solution)/shard_map/swap/pallas_call | solution.py:432
  25.9 0.0 copy-start.1
  25.9 1.6 %copy-done.1 = f32[8,8,64,128]{3,2,1,0:T(8,128)S(1)} copy-done((f32[8,8,64,128]{3,2,1,0:T(8,128)S(1)}, f32[8,8,64,128]{3,2,1,0:T(8,128)}, u32[]{:S(2)}) %copy-start.1) | copy-done | bytes 2097176
  27.5 0.9 copy-done.3
  28.4 0.9 copy-done.5
  29.4 0.9 copy-done.7
  30.3 1.0 copy-done.8
  31.4 0.9 copy-done.10
  32.3 0.8 copy-done.11
  33.1 24.7 %powers.1 = (f32[64,8,40,128]{3,2,1,0:T(8,128)}, f32[16,128]{1,0:T(8,128)S(1)}) custom-call(f32[8,8,64,128]{3,2,1,0:T(8,128)S(1)} %copy-done.1, f32[8,64,128]{2,1,0:T(8,128)S(1)} %copy-done.3, f32[8,64,128]{2,1,0:T(8,128)S(1)} %copy-done.5, f32[2,32,8,128]{3,2,1,0:T(8,128)S(1)} %copy-done.7, f32[2,52,8,128]{3,2,1,0:T(8,128)S(1)} %copy-done.8, ...), custom_call_target="tpu_custom_call" | custom-call | tf_op jit(solution)/shard_map/powers/pallas_call | solution.py:438
  57.8 0.0 copy-start.16
  57.8 0.6 copy-done.16
  58.4 11.2 %sum_1.1.g_ref = f32[16,128]{1,0:T(8,128)} custom-call(f32[16,128]{1,0:T(8,128)} %copy-done.16), custom_call_target="tpu_custom_call" | custom-call | tf_op jit(solution)/shard_map/sum_1/pallas_call | solution.py:366
  69.6 0.0 copy-start.14
  69.6 0.7 copy-done.14
  70.3 17.7 %again.1 = (f32[40,40]{1,0:T(8,128)}, f32[40,40]{1,0:T(8,128)S(1)}, f32[16,128]{1,0:T(8,128)S(1)}) custom-call(f32[16,128]{1,0:T(8,128)S(1)} %copy-done.14, f32[64,8,40,128]{3,2,1,0:T(8,128)} %get-tuple-element.23.k_ref), custom_call_target="tpu_custom_call" | custom-call | tf_op jit(solution)/shard_map/again/pallas_call | solution.py:461
  88.0 0.6 copy-done.17
  88.6 10.4 %sum_2.1.g_ref = f32[16,128]{1,0:T(8,128)} custom-call(f32[16,128]{1,0:T(8,128)} %copy-done.17), custom_call_target="tpu_custom_call" | custom-call | tf_op jit(solution)/shard_map/sum_2/pallas_call | solution.py:366
  99.0 0.0 copy-start.13
  99.0 0.7 copy-done.13
  99.7 0.7 copy-done.15
  100.4 17.8 %basis.1 = (f32[40,8,64,128]{3,2,1,0:T(8,128)}, f32[40,40]{1,0:T(8,128)}) custom-call(f32[16,128]{1,0:T(8,128)S(1)} %copy-done.13, f32[40,40]{1,0:T(8,128)S(1)} %copy-done.15, f32[40,40]{1,0:T(8,128)S(1)} %get-tuple-element.26.inv_ref, f32[64,8,40,128]{3,2,1,0:T(8,128)} %get-tuple-element.23.k_ref), custom_call_target="tpu_custom_call" | custom-call | tf_op jit(solution)/shard_map/basis/pallas_call | solution.py:471
  (11 shorter events, 0.0 us)
Async XLA Ops:
  0.6 1.6 %copy-start = (f32[8,8,64,128]{3,2,1,0:T(8,128)S(1)}, f32[8,8,64,128]{3,2,1,0:T(8,128)}, u32[]{:S(2)}) copy-start(f32[8,8,64,128]{3,2,1,0:T(8,128)} %u_ref.3) | copy-start | bytes 6291460
  2.2 0.9 copy-start.2
  3.2 0.9 copy-start.4
  7.1 0.7 copy-start.6
  7.8 0.8 copy-start.9
  8.6 0.6 copy-start.12
  25.9 1.6 %copy-start.1 = (f32[8,8,64,128]{3,2,1,0:T(8,128)S(1)}, f32[8,8,64,128]{3,2,1,0:T(8,128)}, u32[]{:S(2)}) copy-start(f32[8,8,64,128]{3,2,1,0:T(8,128)} %u_ref.3) | copy-start | bytes 6291460
  27.5 0.9 copy-start.3
  28.4 0.9 copy-start.5
  29.4 0.9 copy-start.7
  30.3 1.0 copy-start.8
  31.4 0.9 copy-start.10
  32.3 0.8 copy-start.11
  57.8 0.6 copy-start.16
  69.6 0.7 copy-start.14
  88.0 0.6 copy-start.17
  99.0 0.7 copy-start.13
  99.7 0.7 copy-start.15
